TPU v7x, 32 devices: a whole 2x2x4 slice. The times are simulated.
32 devices in a mesh: group: 2 (over x), depth: 2 (over core), col: 8 (over z, y).
Axes of the slice: x: 2, y: 2, z: 4, core: 2. Of those that a mesh axis runs over, the one named last changes fastest.
Arguments:
- alignment_activations: bfloat16 [256, 32, 256], P(('group', 'depth'), 'col'), parts along dimension 0, may hold values from -8 to 8
- alignment_mask: int32 [256, 32], P(('group', 'depth'), 'col'), parts along dimension 0, may hold values from 0 to 1, as said below
- pair_activation_input: bfloat16 [64, 32, 128], P(('group', 'col'), 'depth'), parts along dimension 0, may hold values from -6 to 6
- pair_update_mask: int32 [64, 32], P(('group', 'col'), 'depth'), parts along dimension 0, may hold values 0 or 1
- pair_output_gradient: bfloat16 [64, 32, 128], P(('group', 'col'), 'depth'), parts along dimension 0, may hold values from -6 to 6
- layer_scale_factor: float32 [256], replicated, may hold values from 0.25 to 1.75
- first_projector: bfloat16 [256, 32], replicated, may hold values from -0.375 to 0.375
- second_projector: bfloat16 [256, 32], replicated, may hold values from -0.375 to 0.375
- output_weight: bfloat16 [1024, 128], replicated, may hold values from -1.5 to 1.5
- pair_norm_gain: float32 [128], replicated, may hold values from 0.25 to 1.75
- hidden_weight: bfloat16 [128, 512], replicated, may hold values from -0.5 to 0.5
- back_weight: bfloat16 [512, 128], replicated, may hold values from -0.25 to 0.25
Outputs:
- features_derivative: bfloat16 [256, 32, 256], P(('group', 'depth'), 'col'), parts along dimension 0
- couple_features_derivative: bfloat16 [64, 32, 128], P(('group', 'col'), 'depth'), parts along dimension 0
- first_projector_derivative: float32 [512, 32], P('group'), parts along dimension 0
- second_projector_derivative: float32 [512, 32], P('group'), parts along dimension 0
- result_matrix_derivative: float32 [2048, 128], P('group'), parts along dimension 0
- middle_matrix_derivative: float32 [256, 512], P('group'), parts along dimension 0
- final_matrix_derivative: float32 [1024, 128], P('group'), parts along dimension 0
There are 2 independent parts, one for each index of `group`. A program takes and returns all parts, laid end to end along the dimension named above; an argument that names none is the same for every part. Nothing has to cross between parts.
Inputs may be any that keep to these rules, and one draw needn't show every extreme that they name: `alignment_mask`: sequence 0 is present at every residue.
All inputs are finite; a program needn't handle non-finite values. No bound on the sum of `pair_update_mask` on one device may be relied on, other than what follows from the above.
Results may differ from a plain program's by a relative error of at most 0.014.
Values may be sent and summed in bfloat16 or wider, within the bound.
No kernel may reach another device: no remote copies, remote signals or barrier semaphores. Data moves between devices by JAX's collectives and lax.ppermute only.
A program may use at most 64 MiB of HBM per device.

v0:
```python
import jax
import jax.numpy as jnp
from jax import lax
from jax.sharding import PartitionSpec as P

epsilon = 1e-05
highest = lax.Precision.HIGHEST


def norm_pieces(entries_drawn):
    center = entries_drawn - jnp.mean(entries_drawn, axis=-1, keepdims=True)
    inv_std = lax.rsqrt(jnp.mean(center * center, axis=-1, keepdims=True) + epsilon)
    return (center * inv_std, inv_std)


def standardize_adjoint(grad_scaled, scaled, inv_std):
    mean_grad = jnp.mean(grad_scaled, axis=-1, keepdims=True)
    mean_cross = jnp.mean(grad_scaled * scaled, axis=-1, keepdims=True)
    return inv_std * (grad_scaled - mean_grad - scaled * mean_cross)


def silu_pieces(pre_act):
    sigma = jax.nn.sigmoid(pre_act)
    return (pre_act * sigma, sigma * (1.0 + pre_act * (1.0 - sigma)))


def on_device(
    alignment_activations,
    alignment_mask,
    pair_activation_input,
    pair_update_mask,
    pair_output_gradient,
    layer_scale_factor,
    first_projector,
    second_projector,
    output_weight,
    pair_norm_gain,
    hidden_weight,
    back_weight,
):
    sequence_row_block, residue_row_block, channel_total = alignment_activations.shape
    proj_width = first_projector.shape[1]
    outer_width = proj_width * proj_width
    depth_count = lax.axis_size("depth")
    residues = residue_row_block * lax.axis_size("col")
    pair_cols = pair_activation_input.shape[1]
    pair_width = pair_activation_input.shape[2]
    col_block = min(64, pair_cols)
    block_count = pair_cols // col_block
    standardized_features, reciprocal_spread = norm_pieces(
        alignment_activations.astype(jnp.float32)
    )
    normalized_rows = (standardized_features * layer_scale_factor).astype(jnp.bfloat16)
    mask_floating = alignment_mask.astype(jnp.float32)
    left_proj = (
        jnp.dot(normalized_rows, first_projector, preferred_element_type=jnp.float32)
        * mask_floating[:, :, None]
    ).astype(jnp.bfloat16)
    right_proj = (
        jnp.dot(normalized_rows, second_projector, preferred_element_type=jnp.float32)
        * mask_floating[:, :, None]
    ).astype(jnp.bfloat16)
    right_flat = right_proj.reshape(sequence_row_block, residue_row_block * proj_width)
    mask_converted = alignment_mask.astype(jnp.bfloat16)
    seq_total = left_proj.shape[0]
    gathered, gathered_mask = (
        lax.all_gather(right_flat, "col", axis=1, tiled=True),
        lax.all_gather(mask_converted, "col", axis=1, tiled=True),
    )
    right_blocks = gathered.reshape(seq_total, depth_count, pair_cols, proj_width)
    mask_blocks = gathered_mask.reshape(seq_total, depth_count, pair_cols)
    block_depth = right_blocks.shape[1]
    out_wide = output_weight.astype(jnp.float32)

    def partial_outer(col_start):
        right_piece = lax.dynamic_slice_in_dim(right_blocks, col_start, col_block, 2)
        outer_part = jnp.einsum(
            "sic,sejd->iejcd", left_proj, right_piece, preferred_element_type=jnp.float32
        )
        return (
            outer_part.reshape(residue_row_block, block_depth, col_block, outer_width),
            right_piece,
        )

    def forward_step(step_index, loop_state):
        projected, pair_count = loop_state
        col_start = step_index * col_block
        outer_part, right_piece = partial_outer(col_start)
        mask_piece = lax.dynamic_slice_in_dim(mask_blocks, col_start, col_block, 2).astype(
            jnp.float32
        )
        count_part = jnp.einsum("si,sej->iej", mask_floating, mask_piece, precision=highest)
        outer_mine, count_mine = (
            lax.psum_scatter(
                outer_part.astype(jnp.bfloat16), "depth", scatter_dimension=1, tiled=True
            ).astype(jnp.float32),
            lax.psum_scatter(
                count_part.astype(jnp.bfloat16), "depth", scatter_dimension=1, tiled=True
            ).astype(jnp.float32),
        )
        proj_mine = jnp.dot(
            outer_mine.reshape(residue_row_block * col_block, outer_width),
            out_wide,
            precision=highest,
        )
        proj_mine = proj_mine.reshape(residue_row_block, col_block, pair_width)
        count_mine = count_mine.reshape(residue_row_block, col_block)
        projected = lax.dynamic_update_slice_in_dim(projected, proj_mine, col_start, 1)
        pair_count = lax.dynamic_update_slice_in_dim(pair_count, count_mine, col_start, 1)
        return (projected, pair_count)

    projected, pair_count = lax.fori_loop(
        0,
        block_count,
        forward_step,
        (
            jnp.zeros((residue_row_block, pair_cols, pair_width), jnp.float32),
            jnp.zeros((residue_row_block, pair_cols), jnp.float32),
        ),
    )
    count_column = pair_count.reshape(residue_row_block * pair_cols, 1)
    mid_act = (
        pair_activation_input.reshape(residue_row_block * pair_cols, pair_width).astype(jnp.float32)
        + projected.reshape(residue_row_block * pair_cols, pair_width) / count_column
    )
    pair_scaled, pair_inv = norm_pieces(mid_act)
    pair_normed = (pair_scaled * pair_norm_gain).astype(jnp.bfloat16)
    pre_act = jnp.dot(pair_normed, hidden_weight, preferred_element_type=jnp.float32)
    act_value, act_slope = silu_pieces(pre_act)
    hidden = act_value.astype(jnp.bfloat16)
    masked_grad = (
        pair_output_gradient * pair_update_mask.astype(jnp.bfloat16)[:, :, None]
    ).reshape(residue_row_block * pair_cols, pair_width)
    final_matrix_derivative = jnp.dot(hidden.T, masked_grad, preferred_element_type=jnp.float32)
    back_prod = jnp.dot(masked_grad, back_weight.T, preferred_element_type=jnp.float32)
    grad_hidden = (back_prod * act_slope).astype(jnp.bfloat16)
    middle_matrix_derivative = jnp.dot(
        pair_normed.T, grad_hidden, preferred_element_type=jnp.float32
    )
    grad_scaled = (
        jnp.dot(grad_hidden, hidden_weight.T, preferred_element_type=jnp.float32) * pair_norm_gain
    )
    grad_mid = pair_output_gradient.reshape(residue_row_block * pair_cols, pair_width).astype(
        jnp.float32
    ) + standardize_adjoint(grad_scaled, pair_scaled, pair_inv)
    couple_features_derivative = grad_mid.astype(jnp.bfloat16).reshape(
        residue_row_block, pair_cols, pair_width
    )
    grad_opm = (
        (grad_mid / count_column)
        .astype(jnp.bfloat16)
        .reshape(residue_row_block, pair_cols, pair_width)
    )
    full_opm = lax.all_gather(grad_opm, "depth", axis=1, tiled=True).reshape(
        residue_row_block, depth_count, pair_cols, pair_width
    )

    def backward_step(step_index, loop_state):
        grad_left_acc, grad_out, right_term = loop_state
        col_start = step_index * col_block
        outer_part, right_piece = partial_outer(col_start)
        opm_piece = lax.dynamic_slice_in_dim(full_opm, col_start, col_block, 2).reshape(
            residue_row_block * block_depth * col_block, pair_width
        )
        grad_out = grad_out + jnp.dot(
            outer_part.reshape(residue_row_block * block_depth * col_block, outer_width).T,
            opm_piece.astype(jnp.float32),
            precision=highest,
        )
        grad_outer = jnp.dot(opm_piece, output_weight.T, preferred_element_type=jnp.float32).astype(
            jnp.bfloat16
        )
        grad_outer = grad_outer.reshape(
            residue_row_block, block_depth, col_block, proj_width, proj_width
        )
        grad_left_acc = grad_left_acc + jnp.einsum(
            "iejcd,sejd->sic", grad_outer, right_piece, preferred_element_type=jnp.float32
        )
        piece_term = jnp.einsum(
            "iejcd,sic->ejsd", grad_outer, left_proj, preferred_element_type=jnp.float32
        )
        piece_term = piece_term.reshape(block_depth, col_block, seq_total * proj_width)
        right_term = lax.dynamic_update_slice_in_dim(right_term, piece_term, col_start, 1)
        return (grad_left_acc, grad_out, right_term)

    grad_left_acc, result_matrix_derivative, right_term = lax.fori_loop(
        0,
        block_count,
        backward_step,
        (
            jnp.zeros((seq_total, residue_row_block, proj_width), jnp.float32),
            jnp.zeros((outer_width, pair_width), jnp.float32),
            jnp.zeros((block_depth, pair_cols, seq_total * proj_width), jnp.float32),
        ),
    )
    grad_right_sum = lax.psum_scatter(
        right_term.reshape(residues, seq_total * proj_width), "col", scatter_dimension=0, tiled=True
    )
    grad_right_acc = jnp.transpose(
        grad_right_sum.reshape(residue_row_block, seq_total, proj_width), (1, 0, 2)
    )
    grad_left = (grad_left_acc * mask_floating[:, :, None]).astype(jnp.bfloat16)
    grad_right = (grad_right_acc * mask_floating[:, :, None]).astype(jnp.bfloat16)
    normed_rows = normalized_rows.reshape(sequence_row_block * residue_row_block, channel_total)
    first_projector_derivative = jnp.dot(
        normed_rows.T,
        grad_left.reshape(sequence_row_block * residue_row_block, proj_width),
        preferred_element_type=jnp.float32,
    )
    second_projector_derivative = jnp.dot(
        normed_rows.T,
        grad_right.reshape(sequence_row_block * residue_row_block, proj_width),
        preferred_element_type=jnp.float32,
    )
    standardized_derivative = jnp.dot(
        grad_left, first_projector.T, preferred_element_type=jnp.float32
    ) + jnp.dot(grad_right, second_projector.T, preferred_element_type=jnp.float32)
    features_derivative = standardize_adjoint(
        standardized_derivative * layer_scale_factor, standardized_features, reciprocal_spread
    ).astype(jnp.bfloat16)
    weight_sums = lax.psum(
        (
            first_projector_derivative,
            second_projector_derivative,
            result_matrix_derivative,
            middle_matrix_derivative,
            final_matrix_derivative,
        ),
        ("depth", "col"),
    )
    return (
        features_derivative,
        couple_features_derivative,
        weight_sums[0],
        weight_sums[1],
        weight_sums[2],
        weight_sums[3],
        weight_sums[4],
    )


def solution(mesh):
    in_specs = (
        P(("group", "depth"), "col", None),
        P(("group", "depth"), "col"),
        P(("group", "col"), "depth", None),
        P(("group", "col"), "depth"),
        P(("group", "col"), "depth", None),
        P(),
        P(),
        P(),
        P(),
        P(),
        P(),
        P(),
    )
    out_specs = (
        P(("group", "depth"), "col", None),
        P(("group", "col"), "depth", None),
        P("group", None),
        P("group", None),
        P("group", None),
        P("group", None),
        P("group", None),
    )
    return jax.shard_map(
        on_device, mesh=mesh, in_specs=in_specs, out_specs=out_specs, check_vma=False
    )
```

profile of v0, /device:TPU:0, one launch (start us, length us, event | category | flops | bytes accessed | tf_op | source)
XLA Modules:
  0.0 359.8 jit_solution(7298277247969911914)
XLA Ops:
  7.2 1.0 convert_reduce_fusion
  8.3 1.1 fusion.16
  9.4 0.8 convert_bitcast_fusion
  10.2 1.2 fusion.4
  11.3 32.5 %all_gather.9 = bf16[64,1024]{0,1:T(8,128)(2,1)S(1)} all-gather(bf16[64,128]{0,1:T(8,128)(2,1)S(1)} %bitcast.138), channel_id=1, replica_groups=mesh['group'=2,'depth'=2,'col'=8] {'col'}, dimensions={1}, use_global_device_ids=true | all-gather | bytes 147456 | tf_op jit(solution)/shard_map/all_gather | solution.py:67
  43.9 1.2 fusion.5
  45.0 1.8 fusion.45
  46.8 0.6 copy.30
  47.5 1.9 convert_element_type.96
  49.4 20.6 %all-gather = bf16[8,4,64]{2,1,0:T(4,128)(2,1)S(1)} all-gather(bf16[1,4,64]{2,1,0:T(4,128)(2,1)S(1)} %get-tuple-element.95), channel_id=1, replica_groups=mesh['group'=2,'depth'=2,'col'=8] {'col'}, dimensions={0}, use_global_device_ids=true | all-gather | bytes 4608 | tf_op jit(solution)/shard_map/all_gather | solution.py:68
  70.1 2.5 all-reduce.1
  72.6 0.6 dynamic-slice
  73.2 0.7 dynamic-slice_convert_fusion
  74.0 0.6 dynamic-slice.4
  74.6 1.9 copy.35
  76.6 1.0 reshape.170
  78.3 1.6 constant_dynamic-slice_fusion.1
  79.8 0.2 fusion.46
  80.3 0.2 multiply_reduce_fusion.1
  80.9 0.2 fusion.1
  81.0 0.3 fusion.43
  81.3 0.9 fusion.31
  82.2 0.9 fusion.17
  83.2 0.7 fusion.44
  84.0 1.8 all_gather.11
  85.8 0.2 convolution_convert_fusion
  86.0 0.8 reshape.166
  86.8 0.4 convolution_bitcast_fusion.1
  87.3 0.4 fusion.3
  87.7 0.4 copy.33
  88.1 1.2 reshape.167
  89.4 0.9 convolution_bitcast_fusion.4
  90.2 1.4 fusion.47
  91.6 65.7 %all-reduce.12.cloned.1.call-done = f32[32,2048]{1,0:T(8,128)} async-done(((f32[32,2048]{1,0:T(8,128)}), f32[32,2048]{1,0:T(8,128)}) %all-reduce.12.cloned.1.call-update) | async-done | bytes 262160
  157.3 0.8 constant_dynamic-slice_fusion
  158.3 0.9 convolution_bitcast_fusion.3
  159.3 0.2 fusion.24
  159.5 0.3 all-reduce.16.cloned.1.call-update
  159.8 0.3 fusion.42
  160.2 0.2 fusion.15
  160.4 0.8 copy.36
  161.2 84.2 %all-reduce.14.cloned.1.call-done = (f32[256,32]{0,1:T(8,128)}, f32[256,32]{0,1:T(8,128)}) async-done(((f32[256,32]{0,1:T(8,128)}, f32[256,32]{0,1:T(8,128)}), (f32[256,32]{0,1:T(8,128)}, f32[256,32]{0,1:T(8,128)})) %all-reduce.14.cloned.1.call-update) | async-done | bytes 65552 | tf_op jit(solution)/shard_map/psum | solution.py:221
  245.4 99.9 %all-reduce.16.cloned.1.call-done = (f32[1024,128]{1,0:T(8,128)}, f32[128,512]{1,0:T(8,128)}, f32[512,128]{1,0:T(8,128)}) async-done(((f32[1024,128]{1,0:T(8,128)}, f32[128,512]{1,0:T(8,128)}, f32[512,128]{1,0:T(8,128)}), (f32[1024,128]{1,0:T(8,128)}, f32[128,512]{1,0:T(8,128)}, f32[512,128]{1,0:T(8,128)})) %all-reduce.16.cloned.1.call-update) | async-done | bytes 1048592 | tf_op jit(solution)/shard_map/psum | solution.py:221
  345.3 1.4 copy.62
  346.7 1.4 copy.63
  348.1 1.9 copy.64
  350.0 1.7 copy.65
  351.6 1.7 copy.66
  (55 shorter events, 1.4 us)
Async XLA Ops:
  7.2 72.7 %copy-start = (bf16[1024,128]{1,0:T(8,128)(2,1)S(1)}, bf16[1024,128]{1,0:T(8,128)(2,1)}, u32[]{:S(2)}) copy-start(bf16[1024,128]{1,0:T(8,128)(2,1)} %param.20) | copy-start | bytes 786436
  7.2 71.1 %all-reduce.10.cloned.1.call-start = ((), (), s32[]{:S(2)}) async-start(), calls=%async_computation | async-start | bytes 524288
  46.8 23.2 %copy-start.7 = (s32[64,4]{0,1:T(4,128)S(1)}, s32[64,4]{0,1:T(4,128)}, u32[]{:S(2)}) copy-start(s32[64,4]{0,1:T(4,128)} %param.13) | copy-start | bytes 3076
  46.8 25.8 %copy-start.13 = (u32[32]{0:T(128)S(1)}, u32[32]{0:T(128)}, u32[]{:S(2)}) copy-start(u32[32]{0:T(128)} %constant.47) | copy-start | bytes 388
  46.8 27.1 %copy-start.9 = (s32[4,16]{1,0:T(4,128)S(1)}, s32[4,16]{1,0:T(4,128)}, u32[]{:S(2)}) copy-start(s32[4,16]{1,0:T(4,128)} %param.15) | copy-start | bytes 772
  46.8 27.1 %copy-start.12 = (u32[32]{0:T(128)S(1)}, u32[32]{0:T(128)}, u32[]{:S(2)}) copy-start(u32[32]{0:T(128)} %constant.55) | copy-start | bytes 388
  49.4 107.9 %all-reduce.12.cloned.1.call-start = ((), (), s32[]{:S(2)}) async-start(), calls=%async_computation.1 | async-start | bytes 524288
  76.5 1.7 copy-start.4
  76.5 3.5 copy-start.3
  76.5 4.2 %copy-start.2 = (bf16[128,512]{1,0:T(8,128)(2,1)S(1)}, bf16[128,512]{1,0:T(8,128)(2,1)}, u32[]{:S(2)}) copy-start(bf16[128,512]{1,0:T(8,128)(2,1)} %param.22) | copy-start | bytes 393220
  76.5 4.1 %copy-start.8 = (f32[128]{0:T(128)S(1)}, f32[128]{0:T(128)}, u32[]{:S(2)}) copy-start(f32[128]{0:T(128)} %param.21) | copy-start | bytes 1540
  76.6 4.3 %copy-start.11 = (bf16[512,128]{1,0:T(8,128)(2,1)S(1)}, bf16[512,128]{1,0:T(8,128)(2,1)}, u32[]{:S(2)}) copy-start(bf16[512,128]{1,0:T(8,128)(2,1)} %param.23) | copy-start | bytes 393220
  87.2 2.1 copy-start.1
  87.3 2.1 copy-start.10
  88.1 71.2 %copy-start.5 = (bf16[256,32]{0,1:T(8,128)(2,1)S(1)}, bf16[256,32]{0,1:T(8,128)(2,1)}, u32[]{:S(2)}) copy-start(bf16[256,32]{0,1:T(8,128)(2,1)} %param.18) | copy-start | bytes 49156
  89.3 70.6 %copy-start.6 = (bf16[256,32]{0,1:T(8,128)(2,1)S(1)}, bf16[256,32]{0,1:T(8,128)(2,1)}, u32[]{:S(2)}) copy-start(bf16[256,32]{0,1:T(8,128)(2,1)} %param.19) | copy-start | bytes 49156
  89.3 156.1 %all-reduce.14.cloned.1.call-start = ((), (), s32[]{:S(2)}) async-start(), calls=%async_computation.2 | async-start | bytes 131072 | tf_op jit(solution)/shard_map/psum | solution.py:221
  159.2 186.1 %all-reduce.16.cloned.1.call-start = ((), (), s32[]{:S(2)}) async-start(), calls=%async_computation.3 | async-start | bytes 2097152 | tf_op jit(solution)/shard_map/psum | solution.py:221
Sparse Core Ops, SparseCore 0:
  49.5 19.2 all-reduce.9
  89.4 67.8 all-reduce.11
  161.4 83.9 all-reduce.13
  250.1 95.2 all-reduce.15
where the time goes:
time: 360 us
  waiting for transfers between devices  250 us (69%)
  blocking collectives  57.4 us (16%)
  local copies, waits for them, and re-layouts  20.5 us (6%)
  between operations  14.8 us (4%)
  matrix products  11.6 us (3%)
  other arithmetic  5.09 us (1%)
    psum x2, waiting for transfers between devices, on_device(): lax.psum((first_projector_derivative, second_projector_derivative, result...  184 us
    unnamed x6, waiting for transfers between devices  66 us
    all_gather x1, blocking collectives, on_device(): lax.all_gather(right_flat, 'col', axis=1, tiled=True)  32.5 us
    all_gather x1, blocking collectives, on_device(): lax.all_gather(mask_converted, 'col', axis=1, tiled=True)  20.6 us
    unnamed x38, local copies, waits for them, and re-layouts  12.4 us
  transfers between devices with their start and end apart: 4, of which 3 were waited for; matrix products, arithmetic and copies ran while one was open for 2% of the time, Pallas kernels for 0%

commit v1 on v0

--- a/solution.py
+++ b/solution.py
@@ -1,6 +1,10 @@
+import functools
+
 import jax
 import jax.numpy as jnp
 from jax import lax
+from jax.experimental import pallas as pl
+from jax.experimental.pallas import tpu as pltpu
 from jax.sharding import PartitionSpec as P
 
 epsilon = 1e-05
@@ -24,7 +28,7 @@
     return (pre_act * sigma, sigma * (1.0 + pre_act * (1.0 - sigma)))
 
 
-def on_device(
+def split_plan(
     alignment_activations,
     alignment_mask,
     pair_activation_input,
@@ -239,6 +243,483 @@
     )
 
 
+FEW_RESIDUES = 32
+MASK_ROWS = 16
+
+
+def butterfly(blocks, group):
+    lane_group = lax.broadcasted_iota(jnp.int32, blocks[0].shape, 1) // group
+    width = 4 * group
+    for bit in (2, 1):
+        low = (lane_group & bit) == 0
+        swapped = list(blocks)
+        for at in range(4):
+            if at & bit:
+                continue
+            here, there = blocks[at], blocks[at | bit]
+            moving = jnp.where(low, there, here)
+            if bit == 2:
+                moved = pltpu.roll(moving, 2 * group, 1)
+            else:
+                moved = jnp.where(
+                    low, pltpu.roll(moving, width - group, 1), pltpu.roll(moving, group, 1)
+                )
+            swapped[at] = jnp.where(low, here, moved)
+            swapped[at | bit] = jnp.where(low, moved, there)
+        blocks = swapped
+    return blocks
+
+
+def pre_kernel(
+    ids_ref,
+    x_ref,
+    mask_ref,
+    act_ref,
+    pmask_ref,
+    grad_ref,
+    scale_ref,
+    proj_ref,
+    sent_ref,
+    normed_ref,
+    scaled_ref,
+    inv_ref,
+    lanes_ref,
+    wide_ref,
+    tile_ref,
+    turned_ref,
+):
+    seqs, res = mask_ref.shape
+    lanes = proj_ref.shape[1] // 2
+    group = lanes // res
+    pairs = act_ref.shape[0]
+    scaled, inv = norm_pieces(x_ref[...].astype(jnp.float32))
+    scaled_ref[...] = scaled
+    inv_ref[...] = inv
+    normed = (scaled * scale_ref[...]).astype(jnp.bfloat16)
+    normed_ref[...] = normed
+    wide = jnp.dot(normed, proj_ref[...], preferred_element_type=jnp.float32)
+    for at in range(2):
+        wide_ref[at] = wide[:, at * lanes : (at + 1) * lanes]
+    lane_group = lax.broadcasted_iota(jnp.int32, (seqs, lanes), 1) // group
+    mask = mask_ref[...].astype(jnp.float32)
+    both = [jnp.zeros((seqs, lanes), jnp.float32) for _ in range(2)]
+    mask_lanes = jnp.zeros((seqs, lanes), jnp.float32)
+    for r in range(res):
+        mine = lane_group == r
+        both = [
+            jnp.where(mine, wide_ref[at, pl.ds(r, seqs, stride=res), :], both[at])
+            for at in range(2)
+        ]
+        mask_lanes = jnp.where(mine, mask[:, r : r + 1], mask_lanes)
+    lanes_ref[...] = mask_lanes
+    left = (both[0] * mask_lanes).astype(jnp.bfloat16)
+    right = (both[1] * mask_lanes).astype(jnp.bfloat16)
+    spread = (
+        lax.broadcasted_iota(jnp.int32, (seqs, lanes), 1)
+        == lax.broadcasted_iota(jnp.int32, (seqs, lanes), 0) + ids_ref[0] * seqs
+    ).astype(jnp.float32)
+    turned_ref[...] = lax.dot_general(
+        mask_lanes, spread, (((0,), (0,)), ((), ())), preferred_element_type=jnp.float32
+    )
+    tile_ref[...] = jnp.zeros(tile_ref.shape, jnp.float32)
+    tile_ref[0:res, :] = turned_ref[pl.ds(0, res, stride=group), :]
+    tile_ref[res : 2 * res, 0 : pmask_ref.shape[1]] = pmask_ref[...].astype(jnp.float32)
+    tile = tile_ref[...].astype(jnp.bfloat16)
+    act = act_ref[...]
+    grad = grad_ref[...]
+    for at in range(sent_ref.shape[0]):
+        sent_ref[at, 0:seqs, :] = left
+        sent_ref[at, seqs : 2 * seqs, :] = right
+        sent_ref[at, 2 * seqs : 2 * seqs + pairs, :] = act
+        sent_ref[at, 2 * seqs + pairs : 2 * seqs + 2 * pairs, :] = grad
+        sent_ref[at, 2 * seqs + 2 * pairs :, :] = tile
+
+
+def main_kernel(
+    sizes,
+    ids_ref,
+    mine_ref,
+    other_ref,
+    wout_ref,
+    wturn_ref,
+    gain_ref,
+    hid_ref,
+    back_ref,
+    normed_ref,
+    scaled_ref,
+    inv_ref,
+    lanes_ref,
+    scale_ref,
+    proj_ref,
+    couple_ref,
+    part_ref,
+    dout_ref,
+    dhid_ref,
+    dback_ref,
+    feat_ref,
+    got_ref,
+    leftn_ref,
+    rightt_ref,
+    leftt_ref,
+    turn_ref,
+    outer_ref,
+    maskt_ref,
+    cnt_ref,
+    cntl_ref,
+    pml_ref,
+    pm_ref,
+    proj_out_ref,
+    pn_ref,
+    gh_ref,
+    hidden_ref,
+    mg_ref,
+    gmid_ref,
+    gf_ref,
+    grow_ref,
+    gcol_ref,
+    gor_ref,
+    goc_ref,
+    gs_ref,
+):
+    seqs, res, pair_cols, width = sizes
+    depths, cols = got_ref.shape[0], got_ref.shape[1]
+    residues = cols * res
+    lanes = res * width
+    per = res * pair_cols
+    half = residues * pair_cols
+    pairs = depths * half
+    all_seqs = depths * seqs
+    me_depth = ids_ref[0]
+    me_col = ids_ref[1]
+    f32, bf16 = jnp.float32, jnp.bfloat16
+
+    got_ref[me_depth] = mine_ref[...]
+    got_ref[1 - me_depth] = other_ref[...]
+
+    for e in range(depths):
+        for k in range(cols):
+            leftn_ref[e * seqs : (e + 1) * seqs, k * lanes : (k + 1) * lanes] = got_ref[
+                e, k, 0:seqs, :
+            ]
+    for at, out in ((0, leftt_ref), (1, rightt_ref)):
+        for k in range(cols):
+            block = jnp.concatenate(
+                [got_ref[e, k, at * seqs : (at + 1) * seqs, :] for e in range(depths)], axis=0
+            ).astype(f32)
+            turn_ref[k * lanes : (k + 1) * lanes, :] = block.T
+        for d in range(width):
+            out[d * residues : (d + 1) * residues, :] = turn_ref[
+                pl.ds(d, residues, stride=width), :
+            ].astype(bf16)
+
+    base = 2 * seqs + 2 * per
+    pair_lane = lax.broadcasted_iota(jnp.int32, (pair_cols, lanes), 1)
+    pair_row = lax.broadcasted_iota(jnp.int32, (pair_cols, lanes), 0)
+    for k in range(cols):
+        tiles = [got_ref[e, k, base : base + MASK_ROWS, :].astype(f32) for e in range(depths)]
+        maskt_ref[k * res : (k + 1) * res, :] = tiles[0][0:res] + tiles[1][0:res]
+        for e in range(depths):
+            for r in range(res):
+                row = tiles[e][res + r : res + r + 1, :]
+                first = e * half + (k * res + r) * pair_cols
+                pml_ref[first : first + pair_cols, :] = jnp.where(
+                    pair_lane == pair_row, row, 0.0
+                ).astype(bf16)
+    maskt = maskt_ref[...]
+    for e in range(depths):
+        cols_mask = maskt[e * pair_cols : (e + 1) * pair_cols, :]
+        for i in range(residues):
+            first = e * half + i * pair_cols
+            cntl_ref[first : first + pair_cols, :] = (maskt[i : i + 1, :] * cols_mask).astype(bf16)
+    ones = jnp.ones((lanes, lanes), bf16)
+    cnt_ref[...] = jnp.dot(cntl_ref[...], ones, preferred_element_type=f32)
+    pm_ref[...] = jnp.dot(pml_ref[...], ones, preferred_element_type=f32).astype(bf16)
+
+    for dh in range(width // 4):
+        prod = jnp.dot(
+            rightt_ref[dh * 4 * residues : (dh + 1) * 4 * residues, :],
+            leftn_ref[...],
+            preferred_element_type=f32,
+        )
+        for k in range(cols):
+            piece = prod[:, k * lanes : (k + 1) * lanes]
+            turned = butterfly(
+                [piece[a * residues : (a + 1) * residues] for a in range(4)], width
+            )
+            for il in range(res):
+                block = turned[il].astype(bf16)
+                for e in range(depths):
+                    first = e * half + (k * res + il) * pair_cols
+                    outer_ref[first : first + pair_cols, dh * lanes : (dh + 1) * lanes] = block[
+                        e * pair_cols : (e + 1) * pair_cols
+                    ]
+    proj_out_ref[...] = jnp.dot(outer_ref[...], wturn_ref[...], preferred_element_type=f32)
+
+    gain = gain_ref[...]
+    chunk = 2 * per
+    for at in range(pairs // chunk):
+        rows = slice(at * chunk, (at + 1) * chunk)
+        e, k = divmod(2 * at, cols)
+        first = 2 * seqs
+        act = jnp.concatenate(
+            [got_ref[e, k + b, first : first + per, :] for b in range(2)], axis=0
+        ).astype(f32)
+        grad = jnp.concatenate(
+            [got_ref[e, k + b, first + per : first + 2 * per, :] for b in range(2)], axis=0
+        )
+        count = cnt_ref[rows, :]
+        mid = act + proj_out_ref[rows, :] / count
+        scaled, inv = norm_pieces(mid)
+        normed = (scaled * gain).astype(bf16)
+        pn_ref[rows, :] = normed
+        pre = jnp.dot(normed, hid_ref[...], preferred_element_type=f32)
+        value, slope = silu_pieces(pre)
+        hidden_ref[rows, :] = value.astype(bf16)
+        masked = grad * pm_ref[rows, :]
+        mg_ref[rows, :] = masked
+        back = lax.dot_general(
+            masked, back_ref[...], (((1,), (1,)), ((), ())), preferred_element_type=f32
+        )
+        ghid = (back * slope).astype(bf16)
+        gh_ref[rows, :] = ghid
+        gsc = (
+            lax.dot_general(
+                ghid, hid_ref[...], (((1,), (1,)), ((), ())), preferred_element_type=f32
+            )
+            * gain
+        )
+        gmid = grad.astype(f32) + standardize_adjoint(gsc, scaled, inv)
+        gmid_ref[rows, :] = gmid
+        gf_ref[rows, :] = (gmid / count).astype(bf16).astype(f32)
+    start = pl.multiple_of(me_depth * half + me_col * per, per)
+    couple_ref[...] = gmid_ref[pl.ds(start, per), :].astype(bf16)
+
+    for il in range(res):
+        for e in range(depths):
+            first = pl.multiple_of(e * half + (me_col * res + il) * pair_cols, pair_cols)
+            grow_ref[il * residues + e * pair_cols : il * residues + (e + 1) * pair_cols, :] = (
+                gf_ref[pl.ds(first, pair_cols), :].astype(bf16)
+            )
+    my_half = (me_col * res) // pair_cols
+    my_first = me_col * res - my_half * pair_cols
+    for jl in range(res):
+        gcol_ref[jl * residues : (jl + 1) * residues, :] = gf_ref[
+            pl.ds(my_half * half + my_first + jl, residues, stride=pair_cols), :
+        ].astype(bf16)
+    for lhs, weight, out in ((grow_ref, wturn_ref, gor_ref), (gcol_ref, wout_ref, goc_ref)):
+        for dh in range(width // 4):
+            piece = lax.dot_general(
+                lhs[...],
+                weight[dh * lanes : (dh + 1) * lanes, :],
+                (((1,), (1,)), ((), ())),
+                preferred_element_type=f32,
+            )
+            turned = butterfly(
+                [piece[a * residues : (a + 1) * residues] for a in range(4)], width
+            )
+            for dl in range(4):
+                first = (dh * 4 + dl) * residues
+                out[first : first + residues, :] = turned[dl].astype(bf16)
+    sums = [
+        lax.dot_general(lhs[...], rhs[...], (((0,), (0,)), ((), ())), preferred_element_type=f32)
+        for lhs, rhs in ((rightt_ref, gor_ref), (leftt_ref, goc_ref))
+    ]
+    mask_lanes = lanes_ref[...]
+    upper = me_depth == 0
+    sums = [
+        (jnp.where(upper, total[:seqs], total[seqs:]) * mask_lanes).astype(bf16).astype(f32)
+        for total in sums
+    ]
+    lane_group = lax.broadcasted_iota(jnp.int32, (seqs, lanes), 1) // width
+    for r in range(res):
+        for at in range(2):
+            gs_ref[at, pl.ds(r, seqs, stride=res), :] = jnp.where(
+                lane_group == r, sums[at], 0.0
+            )
+    spread = jnp.concatenate([gs_ref[0], gs_ref[1]], axis=1).astype(bf16)
+    cross = lax.dot_general(
+        spread, normed_ref[...], (((0,), (0,)), ((), ())), preferred_element_type=f32
+    )
+    for at in range(2):
+        total = cross[at * lanes : at * lanes + width]
+        for r in range(1, res):
+            total = total + cross[at * lanes + r * width : at * lanes + (r + 1) * width]
+        part_ref[at * width : (at + 1) * width, :] = total
+    back = lax.dot_general(
+        spread, proj_ref[...], (((1,), (1,)), ((), ())), preferred_element_type=f32
+    )
+    feat_ref[...] = standardize_adjoint(
+        back * scale_ref[...], scaled_ref[...], inv_ref[...]
+    ).astype(bf16)
+
+    opm = gf_ref[...].astype(bf16)
+    turn_ref[...] = lax.dot_general(
+        outer_ref[...], opm, (((0,), (0,)), ((), ())), preferred_element_type=f32
+    )
+    for c in range(width):
+        dout_ref[c * width : (c + 1) * width, :] = turn_ref[pl.ds(c, width, stride=width), :]
+    dhid_ref[...] = lax.dot_general(
+        pn_ref[...], gh_ref[...], (((0,), (0,)), ((), ())), preferred_element_type=f32
+    )
+    dback_ref[...] = lax.dot_general(
+        hidden_ref[...], mg_ref[...], (((0,), (0,)), ((), ())), preferred_element_type=f32
+    )
+
+
+def swap_depth(block):
+    return lax.ppermute(block, "depth", [(0, 1), (1, 0)])
+
+
+def pairwise_sum(blocks):
+    while len(blocks) > 1:
+        blocks = [blocks[at] + blocks[at + 1] for at in range(0, len(blocks), 2)]
+    return blocks[0]
+
+
+def whole_plan(
+    alignment_activations,
+    alignment_mask,
+    pair_activation_input,
+    pair_update_mask,
+    pair_output_gradient,
+    layer_scale_factor,
+    first_projector,
+    second_projector,
+    output_weight,
+    pair_norm_gain,
+    hidden_weight,
+    back_weight,
+):
+    seqs, res, channels = alignment_activations.shape
+    width = first_projector.shape[1]
+    outer_width = width * width
+    cols = lax.axis_size("col")
+    depths = lax.axis_size("depth")
+    residues = res * cols
+    pair_cols, pair_width = pair_activation_input.shape[1:]
+    hid = hidden_weight.shape[1]
+    per = res * pair_cols
+    pairs = residues * residues
+    lanes = res * width
+    rows = 2 * seqs + 2 * per + MASK_ROWS
+    f32, bf16 = jnp.float32, jnp.bfloat16
+    ids = jnp.stack([lax.axis_index("depth"), lax.axis_index("col")]).astype(jnp.int32)
+    smem = pl.BlockSpec(memory_space=pltpu.SMEM)
+    vmem = pl.BlockSpec(memory_space=pltpu.VMEM)
+    scale = layer_scale_factor.reshape(1, channels)
+    proj = jnp.concatenate([first_projector] * res + [second_projector] * res, axis=1)
+    wturn = jnp.transpose(output_weight.reshape(width, width, pair_width), (1, 0, 2)).reshape(
+        outer_width, pair_width
+    )
+    shape = jax.ShapeDtypeStruct
+    sent, normed, scaled, inv, mask_lanes = pl.pallas_call(
+        pre_kernel,
+        out_shape=(
+            shape((cols, rows, pair_width), bf16),
+            shape((seqs * res, channels), bf16),
+            shape((seqs * res, channels), f32),
+            shape((seqs * res, 1), f32),
+            shape((seqs, lanes), f32),
+        ),
+        in_specs=[smem] + [vmem] * 7,
+        out_specs=[vmem] * 5,
+        scratch_shapes=[
+            pltpu.VMEM((2, seqs * res, lanes), f32),
+            pltpu.VMEM((MASK_ROWS, lanes), f32),
+            pltpu.VMEM((lanes, lanes), f32),
+        ],
+        compiler_params=pltpu.CompilerParams(vmem_limit_bytes=40 * 2**20),
+        name="project",
+    )(
+        ids,
+        alignment_activations.reshape(seqs * res, channels),
+        alignment_mask,
+        pair_activation_input.reshape(per, pair_width),
+        pair_update_mask,
+        pair_output_gradient.reshape(per, pair_width),
+        scale,
+        proj,
+    )
+    mine = lax.all_to_all(sent, "col", 0, 0)
+    other = swap_depth(mine)
+    couple, part, dout, dhid, dback, feat = pl.pallas_call(
+        functools.partial(main_kernel, (seqs, res, pair_cols, width)),
+        out_shape=(
+            shape((per, pair_width), bf16),
+            shape((2 * width, channels), f32),
+            shape((outer_width, pair_width), f32),
+            shape((pair_width, hid), f32),
+            shape((hid, pair_width), f32),
+            shape((seqs * res, channels), bf16),
+        ),
+        in_specs=[smem] + [vmem] * 13,
+        out_specs=[vmem] * 6,
+        scratch_shapes=[
+            pltpu.VMEM((depths, cols, rows, pair_width), bf16),
+            pltpu.VMEM((depths * seqs, residues * width), bf16),
+            pltpu.VMEM((residues * width, depths * seqs), bf16),
+            pltpu.VMEM((residues * width, depths * seqs), bf16),
+            pltpu.VMEM((residues * width, depths * seqs), f32),
+            pltpu.VMEM((pairs, outer_width), bf16),
+            pltpu.VMEM((residues, depths * seqs), f32),
+            pltpu.VMEM((pairs, lanes), f32),
+            pltpu.VMEM((pairs, lanes), bf16),
+            pltpu.VMEM((pairs, lanes), bf16),
+            pltpu.VMEM((pairs, lanes), bf16),
+            pltpu.VMEM((pairs, pair_width), f32),
+            pltpu.VMEM((pairs, pair_width), bf16),
+            pltpu.VMEM((pairs, hid), bf16),
+            pltpu.VMEM((pairs, hid), bf16),
+            pltpu.VMEM((pairs, pair_width), bf16),
+            pltpu.VMEM((pairs, pair_width), f32),
+            pltpu.VMEM((pairs, pair_width), f32),
+            pltpu.VMEM((res * residues, pair_width), bf16),
+            pltpu.VMEM((res * residues, pair_width), bf16),
+            pltpu.VMEM((residues * width, lanes), bf16),
+            pltpu.VMEM((residues * width, lanes), bf16),
+            pltpu.VMEM((2, seqs * res, lanes), f32),
+        ],
+        compiler_params=pltpu.CompilerParams(vmem_limit_bytes=40 * 2**20),
+        name="pair_work",
+    )(
+        ids,
+        mine,
+        other,
+        output_weight,
+        wturn,
+        pair_norm_gain.reshape(1, pair_width),
+        hidden_weight,
+        back_weight,
+        normed,
+        scaled,
+        inv,
+        mask_lanes,
+        scale,
+        proj,
+    )
+    part = part.reshape(depths * cols, -1, channels)
+    pieces = lax.all_to_all(part, ("depth", "col"), 0, 0)
+    summed = jnp.sum(pieces, axis=0, keepdims=True)
+    total = lax.all_to_all(
+        jnp.broadcast_to(summed, part.shape), ("depth", "col"), 0, 0
+    ).reshape(2 * width, channels)
+    return (
+        feat.reshape(seqs, res, channels),
+        couple.reshape(res, pair_cols, pair_width),
+        total[:width].T,
+        total[width:].T,
+        dout,
+        dhid,
+        dback,
+    )
+
+
+def on_device(alignment_activations, *others):
+    residues = alignment_activations.shape[1] * lax.axis_size("col")
+    plan = whole_plan if residues <= FEW_RESIDUES else split_plan
+    return plan(alignment_activations, *others)
+
+
 def solution(mesh):
     in_specs = (
         P(("group", "depth"), "col", None),

time: 360 us -> 63.3 us (0.18)
  waiting for transfers between devices: 250 us -> 7.82 us
  blocking collectives: 57.4 us -> 32.7 us
  between operations: 14.8 us -> 0.73 us
  local copies, waits for them, and re-layouts: 20.5 us -> 6.81 us
  matrix products: 11.6 us -> 0 us
  Pallas kernels: 0 us -> 11.1 us
  other arithmetic: 5.09 us -> 0.11 us
    psum x2 -> x0, waiting for transfers between devices: 184 us -> none  [on_device(): lax.psum((first_projector_derivative, second_projector_derivative, result...]
    unnamed x6 -> x0, waiting for transfers between devices: 66 us -> none
    all_gather x3 -> x0, blocking collectives: 54.9 us -> none  [the longest x1 32.5 us: on_device(): lax.all_gather(right_flat, 'col', axis=1, tiled=True)]
    all_to_all x0 -> x2, blocking collectives: none -> 32.7 us  [the longest x1 23.2 us: whole_plan(): mine = lax.all_to_all(sent, 'col', 0, 0)]
    dot_general x18 -> x0, matrix products: 11.6 us -> none  [the longest x1 1.8 us: partial_outer(): jnp.einsum('sic,sejd->iejcd', left_proj, right_piece, preferred_element_t...]
    pallas_call x0 -> x2, Pallas kernels: none -> 11.1 us  [the longest x1 10 us: whole_plan(): pl.pallas_call(functools.partial(main_kernel, (seqs, res, pair_cols, widt...]
    unnamed x38 -> x21, local copies, waits for them, and re-layouts: 12.4 us -> 3.84 us
    all_to_all x0 -> x1, waiting for transfers between devices: none -> 5.99 us  [whole_plan(): lax.all_to_all(jnp.broadcast_to(summed, part.shape), ('depth', 'col'), 0, 0)]
  transfers between devices with their start and end apart: 4 -> 2, of which waited for: 3 -> 2; matrix products, arithmetic and copies ran while one was open for 2% -> 1% of each run, Pallas kernels for 0% -> 0%
where the time goes in v1:
time: 63.3 us; the launch traced here: 62.7 us
  blocking collectives  32.7 us (52%)
  Pallas kernels  11.1 us (18%)
  waiting for transfers between devices  7.82 us (12%)
  local copies, waits for them, and re-layouts  6.81 us (11%)
  starting transfers between devices  3.49 us (6%)
  between operations  0.73 us (1%)
    all_to_all x1, blocking collectives, whole_plan(): mine = lax.all_to_all(sent, 'col', 0, 0)  23.2 us
    pallas_call x1, Pallas kernels, whole_plan(): pl.pallas_call(functools.partial(main_kernel, (seqs, res, pair_cols, widt...  10 us
    all_to_all x1, blocking collectives, whole_plan(): pieces = lax.all_to_all(part, ('depth', 'col'), 0, 0)  9.5 us
    all_to_all x1, waiting for transfers between devices, whole_plan(): lax.all_to_all(jnp.broadcast_to(summed, part.shape), ('depth', 'col'), 0, 0)  5.99 us
    unnamed x21, local copies, waits for them, and re-layouts  3.84 us
    all_to_all x1, starting transfers between devices, whole_plan(): lax.all_to_all(jnp.broadcast_to(summed, part.shape), ('depth', 'col'), 0, 0)  3.49 us
    ppermute x1, waiting for transfers between devices, swap_depth(): return lax.ppermute(block, 'depth', [(0, 1), (1, 0)])  1.82 us
  transfers between devices with their start and end apart: 2, of which 2 were waited for; matrix products, arithmetic and copies ran while one was open for 1% of the time, Pallas kernels for 0%

profile of v1, /device:TPU:0, one launch (start us, length us, event | category | flops | bytes accessed | tf_op | source)
XLA Modules:
  0.0 62.7 jit_solution(12074018043395965852)
XLA Ops:
  0.6 0.0 copy-start.8
  0.6 0.8 %copy.27.mask_ref = s32[64,4]{1,0:T(8,128)S(1)} copy(s32[64,4]{0,1:T(4,128)} %param.13) | data formatting | bytes 2048 | tf_op args[1]
  1.5 0.8 %copy.19 = bf16[256,32]{1,0:T(8,128)(2,1)S(1)} copy(bf16[256,32]{0,1:T(8,128)(2,1)} %param.18) | data formatting | bytes 32768 | tf_op args[6]
  2.3 0.8 %copy.23 = bf16[256,32]{1,0:T(8,128)(2,1)S(1)} copy(bf16[256,32]{0,1:T(8,128)(2,1)} %param.19) | data formatting | bytes 32768 | tf_op args[7]
  3.1 0.0 copy-done.8
  3.2 0.1 pad_add_fusion.ids_ref
  3.3 0.0 copy-start.3
  3.3 0.0 copy-start.4
  3.3 0.2 concatenate.3.proj_ref
  3.5 0.0 copy-start.6
  3.5 0.0 copy-start.5
  3.5 0.5 copy-done.3
  4.0 0.0 copy-done.4
  4.0 0.2 copy-done.6
  4.2 0.0 copy-done.5
  4.2 1.1 %project.1 = (bf16[8,272,128]{2,1,0:T(8,128)(2,1)S(1)}, bf16[256,256]{1,0:T(8,128)(2,1)S(1)}, f32[256,256]{1,0:T(8,128)S(1)}, f32[256,1]{1,0:T(8,128)S(1)}, f32[64,128]{1,0:T(8,128)S(1)}) custom-call(s32[2]{0:T(128)S(1)} %pad_add_fusion.ids_ref, bf16[256,256]{1,0:T(8,128)(2,1)S(1)} %reshape.48.x_ref, s32[64,4]{1,0:T(8,128)S(1)} %copy.27.mask_ref, ...), custom_call_target="tpu_custom_call" | custom-call | tf_op jit(solution)/shard_map/project/pallas_call | solution.py:615
  5.3 0.0 copy-start
  5.3 23.2 %all_to_all.15.mine_ref = bf16[8,272,128]{2,1,0:T(8,128)(2,1)S(1)} all-to-all(bf16[8,272,128]{2,1,0:T(8,128)(2,1)S(1)} %get-tuple-element.18), channel_id=1, replica_groups=mesh['group'=2,'depth'=2,'col'=8] {'col'}, dimensions={0} | all-to-all | bytes 1114112 | tf_op jit(solution)/shard_map/all_to_all | solution.py:643
  28.5 0.0 collective-permute-start
  28.5 0.0 copy-done
  28.5 0.0 copy-start.1
  28.5 0.0 copy-start.2
  28.5 0.1 copy.28
  28.6 1.8 %collective-permute-done.other_ref = bf16[8,272,128]{2,1,0:T(8,128)(2,1)S(1)} collective-permute-done((bf16[8,272,128]{2,1,0:T(8,128)(2,1)S(1)}, bf16[8,272,128]{2,1,0:T(8,128)(2,1)S(1)}, u32[]{:S(2)}, u32[]{:S(2)}) %collective-permute-start) | collective-permute-done | bytes 557088 | tf_op jit(solution)/shard_map/ppermute | solution.py:570
  30.4 0.0 copy-start.7
  30.4 0.0 copy-done.1
  30.5 0.0 copy-done.2
  30.5 0.6 %copy-done.7 = f32[128]{0:T(128)S(1)} copy-done((f32[128]{0:T(128)S(1)}, f32[128]{0:T(128)}, u32[]{:S(2)}) %copy-start.7) | copy-done | bytes 536
  31.1 10.0 %pair_work.1 = (bf16[64,128]{1,0:T(8,128)(2,1)}, f32[64,256]{1,0:T(8,128)S(1)}, f32[1024,128]{1,0:T(8,128)}, f32[128,512]{1,0:T(8,128)}, f32[512,128]{1,0:T(8,128)}, /*index=5*/bf16[256,256]{1,0:T(8,128)(2,1)S(1)}) custom-call(s32[2]{0:T(128)S(1)} %pad_add_fusion.ids_ref, bf16[8,272,128]{2,1,0:T(8,128)(2,1)S(1)} %all_to_all.15.mine_ref, ...), custom_call_target="tpu_custom_call" | custom-call | tf_op jit(solution)/shard_map/pair_work/pallas_call | solution.py:645
  41.1 9.5 %all_to_all.16 = f32[16,4,256]{2,1,0:T(4,128)S(1)} all-to-all(f32[16,4,256]{2,1,0:T(4,128)S(1)} %reshape.57), channel_id=1, replica_groups=mesh['group'=2,'depth'=2,'col'=8] {'depth','col'}, dimensions={0} | all-to-all | bytes 131072 | tf_op jit(solution)/shard_map/all_to_all | solution.py:701
  50.7 0.6 %broadcast_in_dim.2 = f32[16,4,256]{2,1,0:T(4,128)} broadcast(f32[4,256]{1,0:T(4,128)S(1)} %reduce_sum.9), dimensions={1,2} | broadcast | bytes 69632 | tf_op jit(solution)/shard_map/broadcast_in_dim | solution.py:704
  51.3 3.5 %all-to-all-start.2 = ((f32[16,4,256]{2,1,0:T(4,128)}), f32[16,4,256]{2,1,0:T(4,128)S(1)}, u32[]{:S(2)}, u32[]{:S(2)}) async-start(f32[16,4,256]{2,1,0:T(4,128)} %broadcast_in_dim.2), calls=%async_computation.2 | async-start | bytes 131072 | tf_op jit(solution)/shard_map/all_to_all | solution.py:703
  54.8 0.7 %reshape.55 = bf16[64,4,256]{2,1,0:T(4,128)(2,1)} reshape(bf16[256,256]{1,0:T(8,128)(2,1)S(1)} %get-tuple-element.23) | data formatting | bytes 262144 | tf_op jit(solution)/shard_map/reshape | solution.py:707
  55.5 6.0 %all-to-all-done.2 = f32[16,4,256]{2,1,0:T(4,128)S(1)} async-done(((f32[16,4,256]{2,1,0:T(4,128)}), f32[16,4,256]{2,1,0:T(4,128)S(1)}, u32[]{:S(2)}, u32[]{:S(2)}) %all-to-all-start.2) | async-done | bytes 65568 | tf_op jit(solution)/shard_map/all_to_all | solution.py:703
  61.5 0.6 %slice.15 = f32[32,256]{1,0:T(8,128)} reshape(f32[8,4,256]{2,1,0:T(4,128)S(1)} %get-tuple-element.29) | data formatting | bytes 65536 | tf_op jit(solution)/shard_map/slice | solution.py:710
  62.1 0.6 %slice.13 = f32[32,256]{1,0:T(8,128)} reshape(f32[8,4,256]{2,1,0:T(4,128)S(1)} %get-tuple-element.30) | data formatting | bytes 65536 | tf_op jit(solution)/shard_map/slice | solution.py:709
  (4 shorter events, 0.1 us)
Async XLA Ops:
  0.6 2.5 %copy-start.8 = (bf16[64,4,256]{2,1,0:T(4,128)(2,1)S(1)}, bf16[64,4,256]{2,1,0:T(4,128)(2,1)}, u32[]{:S(2)}) copy-start(bf16[64,4,256]{2,1,0:T(4,128)(2,1)} %param.12) | copy-start | bytes 393220
  3.3 0.7 %copy-start.3 = (bf16[4,16,128]{2,1,0:T(8,128)(2,1)S(1)}, bf16[4,16,128]{2,1,0:T(8,128)(2,1)}, u32[]{:S(2)}) copy-start(bf16[4,16,128]{2,1,0:T(8,128)(2,1)} %param.14) | copy-start | bytes 49156
  3.3 0.7 %copy-start.4 = (bf16[4,16,128]{2,1,0:T(8,128)(2,1)S(1)}, bf16[4,16,128]{2,1,0:T(8,128)(2,1)}, u32[]{:S(2)}) copy-start(bf16[4,16,128]{2,1,0:T(8,128)(2,1)} %param.16) | copy-start | bytes 49156
  3.5 0.7 %copy-start.6 = (s32[4,16]{1,0:T(4,128)S(1)}, s32[4,16]{1,0:T(4,128)}, u32[]{:S(2)}) copy-start(s32[4,16]{1,0:T(4,128)} %pmask_ref.1) | copy-start | bytes 772
  3.5 0.7 %copy-start.5 = (f32[256]{0:T(256)S(1)}, f32[256]{0:T(256)}, u32[]{:S(2)}) copy-start(f32[256]{0:T(256)} %param.17) | copy-start | bytes 3076
  5.3 23.2 %copy-start = (bf16[1024,128]{1,0:T(8,128)(2,1)S(1)}, bf16[1024,128]{1,0:T(8,128)(2,1)}, u32[]{:S(2)}) copy-start(bf16[1024,128]{1,0:T(8,128)(2,1)} %wout_ref.1) | copy-start | bytes 786436
  28.5 2.0 %collective-permute-start = (bf16[8,272,128]{2,1,0:T(8,128)(2,1)S(1)}, bf16[8,272,128]{2,1,0:T(8,128)(2,1)S(1)}, u32[]{:S(2)}, u32[]{:S(2)}) collective-permute-start(bf16[8,272,128]{2,1,0:T(8,128)(2,1)S(1)} %all_to_all.15.mine_ref), channel_id=1, source_target_pairs={{0,8},{8,0},{1,9},{9,1},{2,10},{10,2},{3,11},{11,3},{4,12},{12,4},... | collective-permute-start | bytes 1671176 | tf_op jit(solution)/shard_map/ppermute | solution.py:570
  28.5 2.0 %copy-start.1 = (bf16[128,512]{1,0:T(8,128)(2,1)S(1)}, bf16[128,512]{1,0:T(8,128)(2,1)}, u32[]{:S(2)}) copy-start(bf16[128,512]{1,0:T(8,128)(2,1)} %hid_ref.1) | copy-start | bytes 393220
  28.5 2.0 %copy-start.2 = (bf16[512,128]{1,0:T(8,128)(2,1)S(1)}, bf16[512,128]{1,0:T(8,128)(2,1)}, u32[]{:S(2)}) copy-start(bf16[512,128]{1,0:T(8,128)(2,1)} %back_ref.1) | copy-start | bytes 393220
  30.4 0.7 %copy-start.7 = (f32[128]{0:T(128)S(1)}, f32[128]{0:T(128)}, u32[]{:S(2)}) copy-start(f32[128]{0:T(128)} %param.21) | copy-start | bytes 1540
  51.3 10.2 %all-to-all-start.2 = ((f32[16,4,256]{2,1,0:T(4,128)}), f32[16,4,256]{2,1,0:T(4,128)S(1)}, u32[]{:S(2)}, u32[]{:S(2)}) async-start(f32[16,4,256]{2,1,0:T(4,128)} %broadcast_in_dim.2), calls=%async_computation.2 | async-start | bytes 131072 | tf_op jit(solution)/shard_map/all_to_all | solution.py:703
